TPU v7x, 512 devices: a whole 4x8x8 slice. The times are simulated.
512 devices in a mesh: grp: 8 (over y_hi, core), dp: 64 (over y_lo, z, x).
Axes of the slice: x: 4, y: 8 (y_hi: 4, y_lo: 2; y = y_hi * 2 + y_lo), z: 8, core: 2. Of those that a mesh axis runs over, the one named last changes fastest.
Arguments:
- teacher_in: bfloat16 [1024, 4096], P('grp', 'dp'), may hold values from -6 to 6
- norm_gain: bfloat16 [4096], P('dp'), may hold values from 0.25 to 1.75
- gate_w: bfloat16 [4096, 4096], P(None, 'dp'), may hold values from -0.09375 to 0.09375
- up_w: bfloat16 [4096, 4096], P(None, 'dp'), may hold values from -0.09375 to 0.09375
- down_w: bfloat16 [4096, 4096], P('dp'), may hold values from -0.09375 to 0.09375
- prev_rows: bfloat16 [4096, 4096], P('dp', 'grp'), may hold values from -6 to 6
- student_in: bfloat16 [65536, 768], P('dp'), may hold values from -6 to 6
- student_w: bfloat16 [768, 4096], P(None, 'grp'), may hold values from -0.21875 to 0.21875
- target_rows: int32 [64, 64, 16], replicated, may hold values from 0 to 63
- counts: int32 [64], replicated, may hold values from 1 to 1024, 33280 in all
Outputs:
- teacher_out: bfloat16 [1024, 4096], P('grp', 'dp')
- grad_w: float32 [768, 4096], P('dp', 'grp')
- loss: float32 [], replicated
Inputs may be any that keep to these rules, and one draw needn't show every extreme that they name: Student token s * 16 + j of index h of dp uses row target_rows[h, s, j] of the rows held by index s of dp.
All inputs are finite; a program needn't handle non-finite values.
Results may differ from a plain program's by a relative error of at most 0.0051.
Values may be sent and summed in bfloat16 or wider, within the bound.
A program may use at most 64 MiB of HBM per device.

v0:
```python
import jax
import jax.numpy as jnp
from jax import lax
from jax.sharding import PartitionSpec as P

D_T = 4096
S_DEV = 1024


def on_device(
    teacher_in,
    norm_gain,
    gate_w,
    up_w,
    down_w,
    prev_rows,
    student_in,
    student_w,
    target_rows,
    counts,
):
    rows_full, gain_full = (
        lax.all_gather(teacher_in, "dp", axis=1, tiled=True),
        lax.all_gather(norm_gain, "dp", axis=0, tiled=True),
    )
    xfull = rows_full.astype(jnp.float32)
    scale = lax.rsqrt(jnp.mean(xfull * xfull, axis=-1, keepdims=True) + 1e-05)
    normed = (xfull * scale * gain_full.astype(jnp.float32)).astype(jnp.bfloat16)
    gate = jnp.dot(normed, gate_w, preferred_element_type=jnp.float32)
    up = jnp.dot(normed, up_w, preferred_element_type=jnp.float32)
    hidden = (jax.nn.silu(gate) * up).astype(jnp.bfloat16)
    mixed = lax.psum_scatter(
        lax.dot_general(
            down_w, hidden, (((0,), (1,)), ((), ())), preferred_element_type=jnp.float32
        ),
        "dp",
        scatter_dimension=0,
        tiled=True,
    )
    teacher_out = (teacher_in.astype(jnp.float32) + mixed.T).astype(jnp.bfloat16)
    myself = lax.axis_index("dp")
    sources = lax.axis_size("dp")
    local_rows = prev_rows.shape[0]
    every_row = lax.all_gather(prev_rows, "dp", axis=0, tiled=True)
    offsets = (jnp.arange(sources, dtype=jnp.int32) * local_rows)[:, None]
    wanted = (target_rows[myself] + offsets).reshape(-1)
    teach = jnp.take(every_row, wanted, axis=0).astype(jnp.float32)
    pred = jnp.dot(student_in, student_w, preferred_element_type=jnp.float32)
    pp, tt, pt = lax.psum(
        (
            jnp.sum(pred * pred, axis=-1),
            jnp.sum(teach * teach, axis=-1),
            jnp.sum(pred * teach, axis=-1),
        ),
        "grp",
    )
    pp = pp + 1e-06
    tt = tt + 1e-06
    inv = lax.rsqrt(pp * tt)
    cosine = pt * inv
    tokens_here = student_in.shape[0]
    valid = (jnp.arange(tokens_here, dtype=jnp.int32) < counts[myself]).astype(jnp.float32)
    loss_part = jnp.sum(valid * (1.0 - cosine)) / jnp.sum(counts).astype(jnp.float32)
    weight = valid * (D_T / S_DEV)
    dpred = ((weight * pt * inv / pp)[:, None] * pred - (weight * inv)[:, None] * teach).astype(
        jnp.bfloat16
    )
    grad_w = lax.psum_scatter(
        lax.dot_general(
            student_in, dpred, (((0,), (0,)), ((), ())), preferred_element_type=jnp.float32
        ),
        "dp",
        scatter_dimension=0,
        tiled=True,
    )
    loss = lax.psum(loss_part, "dp")
    return (teacher_out, grad_w, loss)


def solution(mesh):
    in_specs = (
        P("grp", "dp"),
        P("dp"),
        P(None, "dp"),
        P(None, "dp"),
        P("dp", None),
        P("dp", "grp"),
        P("dp", None),
        P(None, "grp"),
        P(),
        P(),
    )
    out_specs = (P("grp", "dp"), P("dp", "grp"), P())
    return jax.shard_map(
        on_device, mesh=mesh, in_specs=in_specs, out_specs=out_specs, check_vma=False
    )
```

profile of v0, /device:TPU:16, one launch (start us, length us, event | category | flops | bytes accessed | tf_op | source)
XLA Modules:
  0.0 1561.3 jit_solution(9242378964852012066)
XLA Ops:
  7.2 0.0 copy-start
  7.2 0.0 copy-start.3
  7.2 0.0 all-gather.3.cloned.1.call-start
  7.2 0.7 all-gather.3.cloned.1.call-update
  7.9 0.0 all-gather.5.cloned.1.call-start
  8.0 0.7 all-gather.5.cloned.1.call-update
  8.7 0.0 reduce-scatter.5.cloned.1.call-start
  8.7 1.4 fusion.27
  10.7 0.9 dynamic-update-slice
  11.6 166.8 %all-reduce = bf16[4096]{0:T(1024)(128)(2,1)S(1)} all-reduce(bf16[4096]{0:T(1024)(128)(2,1)S(1)} %dynamic-update-slice), channel_id=1, replica_groups=mesh['grp'=8,'dp'=64] {'dp'}, use_global_device_ids=true, to_apply=%add | all-reduce | flops 4096 | bytes 16384
  178.4 136.2 %all-gather.3.cloned.1.call-done = bf16[128,4096]{0,1:T(8,128)(2,1)} async-done(((bf16[128,64]{0,1:T(8,128)(2,1)}), bf16[128,4096]{0,1:T(8,128)(2,1)}) %all-gather.3.cloned.1.call-update) | async-done | bytes 1048592 | tf_op jit(solution)/shard_map/all_gather | solution.py:23
  314.7 0.0 copy-start.1
  314.7 1.9 fusion
  316.6 2.2 fusion.12
  318.8 0.0 copy-done.3
  318.8 0.0 copy-done.1
  318.8 3.7 convolution_bitcast_fusion
  322.4 2.9 copy.29
  325.4 0.0 copy-start.6
  325.4 0.0 reduce-scatter.5.cloned.1.call-update
  325.4 0.0 all-reduce.5.cloned.1.call-start
  325.4 0.7 constant_dynamic-slice_fusion.1
  326.1 0.1 copy.24
  326.2 0.1 squeeze.10
  326.3 0.1 squeeze.9
  326.4 0.1 add.92
  326.5 0.1 add.97
  326.6 0.1 add.93
  326.6 0.0 copy-done.6
  326.6 0.6 dynamic_slice.6
  327.3 293.6 %all-gather.5.cloned.1.call-done = bf16[4096,512]{1,0:T(8,128)(2,1)} async-done(((bf16[64,512]{1,0:T(8,128)(2,1)}), bf16[4096,512]{1,0:T(8,128)(2,1)}) %all-gather.5.cloned.1.call-update) | async-done | bytes 4194320 | tf_op jit(solution)/shard_map/all_gather | solution.py:44
  620.9 6.7 gather_fusion
  627.6 0.0 copy-start.5
  627.6 1.3 copy.26
  628.9 0.0 copy-done
  628.9 0.0 copy-done.5
  628.9 0.0 copy-start.2
  628.9 3.9 fusion.3
  632.8 25.6 %all-reduce.2 = (f32[1024]{0:T(1024)S(1)}, f32[1024]{0:T(1024)S(1)}, f32[1024]{0:T(1024)S(1)}) all-reduce(f32[1024]{0:T(1024)S(1)} %get-tuple-element.14, f32[1024]{0:T(1024)S(1)} %get-tuple-element.13, f32[1024]{0:T(1024)S(1)} %get-tuple-element.12), channel_id=1, replica_groups=mesh['grp'=8,'dp'=64] {'grp'}, use_global_device_ids=true, to_apply=%region_7.8 | all-reduce | flops 3072 | bytes 24576 | tf_op jit(solution)/shard_map/psum | solution.py:49
  658.4 1.3 select_reduce_fusion
  659.6 0.0 copy-done.2
  659.6 0.0 copy-start.4
  659.6 3.8 convolution_bitcast_fusion.1
  663.5 0.0 all-reduce.5.cloned.1.call-update
  663.5 0.6 reduce_sum.59
  664.1 0.0 copy-done.4
  664.1 0.1 copy.23
  665.5 277.1 %reduce-scatter.5.cloned.1.call-done = f32[64,128]{1,0:T(8,128)} async-done(((f32[4096,128]{1,0:T(8,128)}), f32[64,128]{1,0:T(8,128)}) %reduce-scatter.5.cloned.1.call-update) | async-done | bytes 32784
  942.6 0.8 copy.30
  944.1 0.7 copy.27
  944.8 153.7 %psum.31 = f32[]{:T(128)} all-reduce(f32[]{:T(128)S(6)} %div.20), channel_id=1, replica_groups=mesh['grp'=8,'dp'=64] {'dp'}, use_global_device_ids=true, to_apply=%region_11.12 | all-reduce | flops 1 | bytes 8 | tf_op jit(solution)/shard_map/psum | solution.py:76
  1098.5 454.4 %all-reduce.5.cloned.1.call-done = f32[768,512]{0,1:T(8,128)} async-done(((f32[768,512]{0,1:T(8,128)}), f32[768,512]{0,1:T(8,128)}) %all-reduce.5.cloned.1.call-update) | async-done | bytes 1572880
  1552.9 1.2 constant_dynamic-slice_fusion
  1554.0 0.7 copy.28
  (8 shorter events, 0.1 us)
Async XLA Ops:
  7.2 621.8 %copy-start = (bf16[1024,768]{1,0:T(8,128)(2,1)S(1)}, bf16[1024,768]{1,0:T(8,128)(2,1)}, u32[]{:S(2)}) copy-start(bf16[1024,768]{1,0:T(8,128)(2,1)} %param.16) | copy-start | bytes 4718596
  7.2 311.6 %copy-start.3 = (bf16[64,4096]{1,0:T(8,128)(2,1)S(1)}, bf16[64,4096]{1,0:T(8,128)(2,1)}, u32[]{:S(2)}) copy-start(bf16[64,4096]{1,0:T(8,128)(2,1)} %param.14) | copy-start | bytes 1572868
  7.2 307.5 %all-gather.3.cloned.1.call-start = ((), (), s32[]{:S(2)}) async-start(), calls=%async_computation.1 | async-start | bytes 1064960 | tf_op jit(solution)/shard_map/all_gather | solution.py:23
  7.9 612.9 %all-gather.5.cloned.1.call-start = ((), (), s32[]{:S(2)}) async-start(), calls=%async_computation.2 | async-start | bytes 4259840 | tf_op jit(solution)/shard_map/all_gather | solution.py:44
  8.7 933.9 %reduce-scatter.5.cloned.1.call-start = ((), (), s32[]{:S(2)}) async-start(), calls=%async_computation.3 | async-start | bytes 2129920
  314.7 4.1 copy-start.1
  325.4 1.3 copy-start.6
  325.4 1227.5 %all-reduce.5.cloned.1.call-start = ((), (), s32[]{:S(2)}) async-start(), calls=%async_computation.4 | async-start | bytes 3145728
  627.6 1.4 copy-start.5
  628.9 30.7 %copy-start.2 = (bf16[1024,512]{0,1:T(8,128)(2,1)S(1)}, bf16[1024,512]{0,1:T(8,128)(2,1)}, u32[]{:S(2)}) copy-start(bf16[1024,512]{0,1:T(8,128)(2,1)} %copy.26) | copy-start | bytes 3145732
  659.6 4.5 copy-start.4
Sparse Core Ops, SparseCore 0:
  10.1 304.5 all-gather.2
  316.8 304.0 all-gather.4
  623.7 318.9 reduce-scatter.4
  945.6 607.2 all-reduce.4
where the time goes:
time: 1560 us
  waiting for transfers between devices  1160 us (74%)
  blocking collectives  346 us (22%)
  local copies, waits for them, and re-layouts  18.6 us (1%)
  between operations  16.5 us (1%)
    unnamed x6, waiting for transfers between devices  733 us
    all_gather x1, waiting for transfers between devices, on_device(): every_row = lax.all_gather(prev_rows, 'dp', axis=0, tiled=True)  294 us
    unnamed x1, blocking collectives  167 us
    psum x1, blocking collectives, on_device(): loss = lax.psum(loss_part, 'dp')  154 us
    all_gather x1, waiting for transfers between devices, on_device(): lax.all_gather(teacher_in, 'dp', axis=1, tiled=True)  136 us
  transfers between devices with their start and end apart: 4, of which 4 were waited for; matrix products, arithmetic and copies ran while one was open for 2% of the time, Pallas kernels for 0%

commit v1 on v0

v1 whole, which is shorter than its diff:
```python
import functools

import jax
import jax.numpy as jnp
from jax import lax
from jax.experimental import pallas as pl
from jax.experimental.pallas import tpu as pltpu
from jax.sharding import PartitionSpec as P

NY = 2
CAP = 16
MESH = pl.DeviceIdType.MESH
F32 = jnp.float32
BF16 = jnp.bfloat16

XG_Z, SS_Z, ROWS_Z, XG_P, SS_P, ROWS_P, STATS, MIX_P, MIX_Z, GRAD_P, GRAD_Z, LOSS_P, LOSS_Z = range(13)
STAGES = 13


def dot(a, b, ca, cb):
    return lax.dot_general(a, b, (((ca,), (cb,)), ((), ())), preferred_element_type=F32)


def iota(shape, axis):
    return lax.broadcasted_iota(jnp.int32, shape, axis)


def kernel(
    nz, nx,
    tin, gain, rows, gate_h, up_h, down_h, x_h, w_h, tr_h, counts,
    tout, gout, loss_out,
    gu, down, xv, wv, tr, xf, xn, ss1, ss2, ssz, ssp, rz, sel, tts, tta, wt, xt, pred, stat, stats, dpt,
    grad, gs, gr, gacc, gzf, gz, gzr, loss1, loss2, lossp, lossz, mix, mixb, mr, mzf, mz, mzr,
    send, recv, local,
):
    nk = NY * nx
    ndp = nk * nz
    groups = lax.axis_size("grp")
    g, dp = lax.axis_index("grp"), lax.axis_index("dp")
    y, z, x = dp // (nz * nx), (dp // nx) % nz, dp % nx
    me = y * nx + x
    nfeat, ntok = tin.shape
    trows, width = rows.shape
    ds = wv.shape[0]
    cap_z = nz * CAP
    tokens = cap_z * nk
    part = ds // nk
    out_rows = part // nz

    def z_peer(d):
        zz = (z + d) % nz
        return zz, (g, (y * nz + zz) * nx + x)

    def p_peer(d):
        yy, xx = (y + d // nx) % NY, (x + d % nx) % nx
        return yy, xx, (g, (yy * nz + z) * nx + xx)

    def p_source(d):
        return (y + NY - d // nx) % NY, (x + nx - d % nx) % nx

    def g_peer(d):
        return ((g + d) % groups, dp)

    def rcopy(src, dst, stage, d, device):
        return pltpu.make_async_remote_copy(
            src_ref=src, dst_ref=dst, send_sem=send.at[stage, d], recv_sem=recv.at[stage, d],
            device_id=device, device_id_type=MESH,
        )

    started = []

    def start(*args):
        copy = rcopy(*args)
        copy.start()
        started.append(copy)

    def arrived(ref, stage, d):
        rcopy(ref, ref, stage, d, z_peer(1)[1]).wait_recv()

    loads = []

    def load(src, dst):
        copy = pltpu.make_async_copy(src, dst, local.at[len(loads)])
        copy.start()
        loads.append(copy)

    for yy in range(NY):
        load(tr_h.at[yy, z], tr.at[pl.ds(yy * nx, nx)])
    load(w_h, wv)
    for d in range(nk):
        yy, xx = p_source(d)
        load(x_h.at[yy, :, xx], xv.at[d])
    load(gate_h, gu.at[pl.ds(0, nfeat)])
    load(up_h, gu.at[pl.ds(nfeat, nfeat)])
    load(down_h, down)

    rz[0] = rows[...]
    xin = tin[...].astype(F32)
    eye = iota((nfeat, nfeat), 0) == iota((nfeat, nfeat), 1)
    gain_col = jnp.sum(jnp.where(eye, gain[...].astype(F32), 0.0), axis=1, keepdims=True)
    xf[0, 0] = (xin * gain_col).astype(BF16)
    ss1[...] = jnp.sum((xin * xin).reshape(nfeat // 8, 8, ntok), axis=0)

    barrier = pltpu.get_barrier_semaphore()
    peers = (
        [z_peer(d)[1] for d in range(1, nz)]
        + [p_peer(d)[2] for d in range(1, nk)]
        + [g_peer(d) for d in range(1, groups)]
    )
    for device in peers:
        pl.semaphore_signal(barrier, inc=1, device_id=device, device_id_type=MESH)
    pl.semaphore_wait(barrier, len(peers))

    for d in range(1, nz):
        start(rz.at[0], rz.at[d], ROWS_Z, d, z_peer(d)[1])
    for d in range(1, nz):
        start(xf.at[0, 0], xf.at[0, d], XG_Z, d, z_peer(d)[1])
        start(ss1, ssz.at[d], SS_Z, d, z_peer(d)[1])

    for copy in loads[:NY]:
        copy.wait()
    pick = (iota((ndp, cap_z), 0) == (y * nz + lax.shift_right_logical(iota((ndp, cap_z), 1), 4)) * nx + x)
    slots = dot(tr[...].reshape(nk * CAP, ndp).astype(F32).astype(BF16), pick.astype(F32).astype(BF16), 1, 0)
    mine = iota((nk, CAP, cap_z), 1) == (iota((nk, CAP, cap_z), 2) & (CAP - 1))
    target = jnp.sum(jnp.where(mine, slots.reshape(nk, CAP, cap_z), 0.0), axis=1)
    slot_z = (z + nz - lax.shift_right_logical(iota((nk, cap_z), 1), 4)) & (nz - 1)
    sel[...] = target.astype(jnp.int32) + slot_z * trows

    for copy in loads[NY : NY + 1 + nk]:
        copy.wait()
    wt[...] = wv[...].T
    for k in range(nk):
        p = dot(wt[...], xv[k].reshape(cap_z, ds), 1, 1)
        pred[k] = p
        stat[0, k : k + 1, :] = jnp.sum(p * p, axis=0, keepdims=True)

    for d in range(1, nz):
        arrived(rz.at[d], ROWS_Z, d)
    rz_t = rz[...].reshape(nz * trows, width).T
    row_of = iota((nz * trows, cap_z), 0)
    for d in list(range(1, nk)) + [0]:
        yy, xx, device = p_peer(d)
        onehot = (row_of == sel[pl.ds(yy * nx + xx, 1), :]).astype(F32).astype(BF16)
        picked = dot(rz_t, onehot, 1, 0).astype(BF16)
        if d == 0:
            tta[0] = picked
        else:
            tts[d] = picked
            start(tts.at[d], tta.at[d], ROWS_P, d, device)

    for d in range(1, nz):
        arrived(xf.at[0, d], XG_Z, d)
        arrived(ssz.at[d], SS_Z, d)
    squares = ss1[...]
    for d in range(1, nz):
        squares += ssz[d]
    ss2[...] = squares
    for d in range(1, nk):
        device = p_peer(d)[2]
        start(xf.at[0], xf.at[d], XG_P, d, device)
        start(ss2, ssp.at[d], SS_P, d, device)

    r = iota((ds, 1), 0).astype(F32)
    rk = jnp.floor((r + 0.5) / part)
    rz_ = jnp.floor((r - rk * part + 0.5) / out_rows)
    ry = jnp.floor((rk + 0.5) / nx)
    column = ((ry * nz + rz_) * nx + (rk - ry * nx)) * out_rows + (r - rk * part - rz_ * out_rows)
    order = (column == iota((ds, ds), 1).astype(F32)).astype(F32).astype(BF16)
    for k in range(nk):
        xt[:, k * cap_z : (k + 1) * cap_z] = dot(order, xv[k].reshape(cap_z, ds), 1, 1).astype(BF16)

    for d in range(nk):
        if d:
            arrived(tta.at[d], ROWS_P, d)
        t = tta[d].astype(F32)
        stat[1, d : d + 1, :] = jnp.sum(t * t, axis=0, keepdims=True)
        stat[2, d : d + 1, :] = jnp.sum(t * pred[d], axis=0, keepdims=True)
    for d in range(1, groups):
        start(stat, stats.at[d], STATS, d, g_peer(d))

    for d in range(1, nk):
        arrived(xf.at[d], XG_P, d)
        arrived(ssp.at[d], SS_P, d)
    for d in range(1, nk):
        squares += ssp[d]
    total = jnp.sum(squares, axis=0, keepdims=True)
    scale = lax.rsqrt(total * (1.0 / (ndp * nfeat)) + 1e-05)
    for copy in loads[NY + 1 + nk :]:
        copy.wait()
    for d in range(nk):
        yy, xx = p_source(d)
        for dz in range(nz):
            xn[yy * nz + (z + nz - dz) % nz, xx] = xf[d, dz]
    h = dot(gu[...], xn[...].reshape(ndp * nfeat, ntok), 1, 0)
    gate, up = h[:nfeat] * scale, h[nfeat:] * scale
    hidden = (gate * jax.nn.sigmoid(gate) * up).astype(BF16)
    per_y = nz * nx * nfeat
    for yy in range(NY):
        m = dot(down[:, yy * per_y : (yy + 1) * per_y], hidden, 0, 0).reshape(nz, nx, nfeat, ntok)
        mix[pl.ds(yy * nz, nz)] = m
        for xx in range(nx):
            mixb[xx, pl.ds(yy * nz, nz)] = m[:, xx].astype(BF16)
    for d in range(1, nk):
        yy, xx, device = p_peer(d)
        start(mixb.at[xx, pl.ds(yy * nz, nz)], mr.at[d], MIX_P, d, device)

    for d in range(1, groups):
        arrived(stats.at[d], STATS, d)
    sums = stat[...]
    for d in range(1, groups):
        sums += stats[d]
    pp, tt, pt = sums[0] + 1e-06, sums[1] + 1e-06, sums[2]
    inv = lax.rsqrt(pp * tt)
    kk, lane = iota((nk, cap_z), 0), iota((nk, cap_z), 1)
    ky = (y + NY - lax.shift_right_logical(kk, nx.bit_length() - 1)) & (NY - 1)
    kx = (x + nx - (kk & (nx - 1))) & (nx - 1)
    source = (ky * nz + lax.shift_right_logical(lane, 4)) * nx + kx
    valid = (source * CAP + (lane & (CAP - 1)) < counts[dp]).astype(F32)
    weight = valid * (ndp * nfeat / tokens)
    count = lax.fori_loop(0, ndp, lambda i, c: c + counts[i], jnp.int32(0))
    loss1[...] = valid * (1.0 - pt * inv)
    for d in range(1, nk):
        start(loss1, lossp.at[d], LOSS_P, d, p_peer(d)[2])
    a, b = weight * pt * inv / pp, weight * inv
    for k in range(nk):
        dpt[:, k * cap_z : (k + 1) * cap_z] = (
            a[k : k + 1] * pred[k] - b[k : k + 1] * tta[k].astype(F32)
        ).astype(BF16)
    gw = dot(xt[...], dpt[...], 1, 1).reshape(nk, part, width)
    grad[...] = gw
    gs[...] = gw.astype(BF16)
    for d in range(1, nk):
        yy, xx, device = p_peer(d)
        start(gs.at[yy * nx + xx], gr.at[d], GRAD_P, d, device)

    for d in range(1, nk):
        arrived(mr.at[d], MIX_P, d)
    m = mix[pl.ds(y * nz, nz), x]
    for d in range(1, nk):
        m += mr[d].astype(F32)
    mzf[...] = m
    mz[...] = m.astype(BF16)
    for d in range(1, nz):
        zz, device = z_peer(d)
        start(mz.at[zz], mzr.at[d], MIX_Z, d, device)

    for d in range(1, nk):
        arrived(lossp.at[d], LOSS_P, d)
    part_loss = loss1[...]
    for d in range(1, nk):
        part_loss += lossp[d]
    loss2[...] = part_loss
    for d in range(1, nz):
        start(loss2, lossz.at[d], LOSS_Z, d, z_peer(d)[1])

    for d in range(1, nk):
        arrived(gr.at[d], GRAD_P, d)
    acc = grad[me]
    for d in range(1, nk):
        acc += gr[d].astype(F32)
    gacc[pl.ds(0, part)] = acc
    gacc[pl.ds(part, 16)] = jnp.zeros((16, width), F32)
    for zz in range(nz):
        piece = gacc[pl.ds(zz * out_rows, 16)]
        gzf[zz] = piece
        gz[zz] = piece.astype(BF16)
    for d in range(1, nz):
        zz, device = z_peer(d)
        start(gz.at[zz], gzr.at[d], GRAD_Z, d, device)

    m = xin + mzf[z]
    for d in range(1, nz):
        arrived(mzr.at[d], MIX_Z, d)
        m += mzr[d].astype(F32)
    tout[...] = m.astype(BF16)

    for d in range(1, nz):
        arrived(lossz.at[d], LOSS_Z, d)
        part_loss += lossz[d]
    loss_out[0, 0] = jnp.sum(part_loss) / count.astype(F32)

    acc = gzf[z]
    for d in range(1, nz):
        arrived(gzr.at[d], GRAD_Z, d)
        acc += gzr[d].astype(F32)
    gout[...] = acc[:out_rows]

    for copy in started:
        copy.wait_send()


def on_device(
    nz, nx, teacher_in, norm_gain, gate_w, up_w, down_w, prev_rows, student_in, student_w, target_rows, counts
):
    nk = NY * nx
    ndp = nk * nz
    ntok, nfeat = teacher_in.shape
    trows, width = prev_rows.shape
    s_dev, ds = student_in.shape
    groups = lax.axis_size("grp")
    cap_z = nz * CAP
    part = ds // nk
    out_rows = part // nz
    d_model = ndp * nfeat
    vm = pl.BlockSpec(memory_space=pltpu.VMEM)
    hbm = pl.BlockSpec(memory_space=pl.ANY)
    sm = pl.BlockSpec(memory_space=pltpu.SMEM)
    v = pltpu.VMEM
    scratch = [
        v((2 * nfeat, d_model), BF16),
        v((nfeat, d_model), BF16),
        v((nk, nz, CAP, ds), BF16),
        v((ds, width), BF16),
        v((nk, CAP, ndp), jnp.int32),
        v((nk, nz, nfeat, ntok), BF16),
        v((NY * nz, nx, nfeat, ntok), BF16),
        v((8, ntok), F32),
        v((8, ntok), F32),
        v((nz, 8, ntok), F32),
        v((nk, 8, ntok), F32),
        v((nz, trows, width), BF16),
        v((nk, cap_z), jnp.int32),
        v((nk, width, cap_z), BF16),
        v((nk, width, cap_z), BF16),
        v((width, ds), BF16),
        v((ds, s_dev), BF16),
        v((nk, width, cap_z), F32),
        v((3, nk, cap_z), F32),
        v((groups, 3, nk, cap_z), F32),
        v((width, s_dev), BF16),
        v((nk, part, width), F32),
        v((nk, part, width), BF16),
        v((nk, part, width), BF16),
        v((part + 16, width), F32),
        v((nz, 16, width), F32),
        v((nz, 16, width), BF16),
        v((nz, 16, width), BF16),
        v((nk, cap_z), F32),
        v((nk, cap_z), F32),
        v((nk, nk, cap_z), F32),
        v((nz, nk, cap_z), F32),
        v((NY * nz, nx, nfeat, ntok), F32),
        v((nx, NY * nz, nfeat, ntok), BF16),
        v((nk, nz, nfeat, ntok), BF16),
        v((nz, nfeat, ntok), F32),
        v((nz, nfeat, ntok), BF16),
        v((nz, nfeat, ntok), BF16),
        pltpu.SemaphoreType.DMA((STAGES, max(nk, nz, groups))),
        pltpu.SemaphoreType.DMA((STAGES, max(nk, nz, groups))),
        pltpu.SemaphoreType.DMA((NY + 4 + nk,)),
    ]
    tout, gout, loss = pl.pallas_call(
        functools.partial(kernel, nz, nx),
        out_shape=(
            jax.ShapeDtypeStruct((nfeat, ntok), BF16),
            jax.ShapeDtypeStruct((out_rows, width), F32),
            jax.ShapeDtypeStruct((1, 1), F32),
        ),
        in_specs=[vm, vm, vm, hbm, hbm, hbm, hbm, hbm, hbm, sm],
        out_specs=(vm, vm, sm),
        scratch_shapes=scratch,
        compiler_params=pltpu.CompilerParams(
            collective_id=0, has_side_effects=True, vmem_limit_bytes=52 * 1024 * 1024
        ),
        name="distill",
    )(
        teacher_in.T,
        norm_gain.reshape(1, nfeat),
        prev_rows,
        gate_w.T,
        up_w.T,
        down_w,
        student_in.reshape(NY, nz, nx, CAP, ds),
        student_w,
        target_rows.transpose(0, 2, 1).reshape(NY, nz, nx, CAP, ndp),
        counts,
    )
    return tout.T, gout, loss.reshape(())


def solution(mesh):
    in_specs = (
        P("grp", "dp"),
        P("dp"),
        P(None, "dp"),
        P(None, "dp"),
        P("dp", None),
        P("dp", "grp"),
        P("dp", None),
        P(None, "grp"),
        P(),
        P(),
    )
    out_specs = (P("grp", "dp"), P("dp", "grp"), P())
    nx = 4
    nz = mesh.shape["dp"] // (NY * nx)
    return jax.shard_map(
        functools.partial(on_device, nz, nx), mesh=mesh, in_specs=in_specs, out_specs=out_specs, check_vma=False
    )
```

time: 1560 us -> 95.8 us (0.06)
  the two profiles are of different devices: /device:TPU:16 before, /device:TPU:2 now
where the time goes in v1:
time: 95.8 us; the launch traced here: 95.4 us
  Pallas kernels  85.9 us (90%)
  local copies, waits for them, and re-layouts  7.2 us (8%)
  between operations  2.35 us (2%)
    pallas_call x1, Pallas kernels, on_device(): pl.pallas_call(functools.partial(kernel, nz, nx), out_shape=(jax.ShapeDty...  85.9 us
    unnamed x16, local copies, waits for them, and re-layouts  7.2 us

profile of v1, /device:TPU:2, one launch (start us, length us, event | category | flops | bytes accessed | tf_op | source)
XLA Modules:
  0.0 95.4 jit_solution(3722308958288351300)
XLA Ops:
  0.6 0.0 copy-start
  0.6 1.0 %copy-done = bf16[4096,64]{0,1:T(8,128)(2,1)S(1)} copy-done((bf16[4096,64]{0,1:T(8,128)(2,1)S(1)}, bf16[4096,64]{0,1:T(8,128)(2,1)}, u32[]{:S(2)}) %copy-start) | copy-done | bytes 524312
  1.7 0.0 copy-start.1
  1.7 1.0 %copy-done.1 = bf16[4096,64]{0,1:T(8,128)(2,1)S(1)} copy-done((bf16[4096,64]{0,1:T(8,128)(2,1)S(1)}, bf16[4096,64]{0,1:T(8,128)(2,1)}, u32[]{:S(2)}) %copy-start.1) | copy-done | bytes 524312
  2.7 0.0 copy-start.2
  2.7 1.0 %copy-done.2 = bf16[64,4096]{1,0:T(8,128)(2,1)S(1)} copy-done((bf16[64,4096]{1,0:T(8,128)(2,1)S(1)}, bf16[64,4096]{1,0:T(8,128)(2,1)}, u32[]{:S(2)}) %copy-start.2) | copy-done | bytes 524312
  3.8 0.0 copy-start.3
  3.8 0.8 copy-done.3
  4.6 0.0 copy-start.4
  4.6 0.7 copy-done.4
  5.3 0.0 copy-start.5
  5.3 0.7 copy-done.5
  6.0 0.0 copy-start.6
  6.0 0.7 copy-done.6
  6.6 85.9 %distill.1 = (bf16[64,128]{1,0:T(8,128)(2,1)S(1)}, f32[12,512]{1,0:T(8,128)S(1)}, f32[1,1]{1,0:T(1,128)}) custom-call(bf16[64,128]{1,0:T(8,128)(2,1)S(1)} %bitcast.12, bf16[1,64]{1,0:T(2,128)(2,1)S(1)} %bitcast.14, bf16[64,512]{1,0:T(8,128)(2,1)S(1)} %copy-done.3, bf16[64,4096]{1,0:T(8,128)(2,1)S(1)} %bitcast.10, bf16[64,4096]{1,0:T(8,128)(2,1)S(1)} %bitcast.11, ...), custom_call_target="tpu_custom_call" | custom-call | tf_op jit(solution)/shard_map/distill/pallas_call | solution.py:352
  92.5 0.6 copy.16
  93.1 0.6 copy.17
Async XLA Ops:
  0.6 1.0 %copy-start = (bf16[4096,64]{0,1:T(8,128)(2,1)S(1)}, bf16[4096,64]{0,1:T(8,128)(2,1)}, u32[]{:S(2)}) copy-start(bf16[4096,64]{0,1:T(8,128)(2,1)} %param.12) | copy-start | bytes 1572868
  1.7 1.0 %copy-start.1 = (bf16[4096,64]{0,1:T(8,128)(2,1)S(1)}, bf16[4096,64]{0,1:T(8,128)(2,1)}, u32[]{:S(2)}) copy-start(bf16[4096,64]{0,1:T(8,128)(2,1)} %param.13) | copy-start | bytes 1572868
  2.7 1.0 %copy-start.2 = (bf16[64,4096]{1,0:T(8,128)(2,1)S(1)}, bf16[64,4096]{1,0:T(8,128)(2,1)}, u32[]{:S(2)}) copy-start(bf16[64,4096]{1,0:T(8,128)(2,1)} %down_h.1) | copy-start | bytes 1572868
  3.8 0.8 copy-start.3
  4.6 0.7 copy-start.4
  5.3 0.7 copy-start.5
  6.0 0.7 copy-start.6

commit v2 on v1

--- a/solution.py
+++ b/solution.py
@@ -13,8 +13,11 @@
 F32 = jnp.float32
 BF16 = jnp.bfloat16
 
-XG_Z, SS_Z, ROWS_Z, XG_P, SS_P, ROWS_P, STATS, MIX_P, MIX_Z, GRAD_P, GRAD_Z, LOSS_P, LOSS_Z = range(13)
-STAGES = 13
+(
+    XA_P, XA_Z, XB_Z, XB_P, SS_Z, SS_P, ROWS_Z0, ROWS_Z1, ROWS_P0, ROWS_P1, STATS,
+    MA_P, MA_Z, MB_Z, MB_P, GRAD_P, GRAD_Z, LOSS_P, LOSS_Z,
+) = range(19)
+STAGES = 19
 
 
 def dot(a, b, ca, cb):
@@ -29,8 +32,9 @@
     nz, nx,
     tin, gain, rows, gate_h, up_h, down_h, x_h, w_h, tr_h, counts,
     tout, gout, loss_out,
-    gu, down, xv, wv, tr, xf, xn, ss1, ss2, ssz, ssp, rz, sel, tts, tta, wt, xt, pred, stat, stats, dpt,
-    grad, gs, gr, gacc, gzf, gz, gzr, loss1, loss2, lossp, lossz, mix, mixb, mr, mzf, mz, mzr,
+    gu, down, xv, wv, tr, xa, xb, xn, ss1, ss2, ssz, ssp, rz, hot, tts, tta, wt, xt, pred, stat, stats, dpt,
+    grad, gs, gr, gacc, gzf, gz, gzr, loss1, loss2, lossp, lossz,
+    mix, mixa, mixb, mra, mrb, mfa, mfb, m2a, m2b, mr2a, mr2b,
     send, recv, local,
 ):
     nk = NY * nx
@@ -46,6 +50,7 @@
     tokens = cap_z * nk
     part = ds // nk
     out_rows = part // nz
+    half, fh = width // 2, nfeat // 2
 
     def z_peer(d):
         zz = (z + d) % nz
@@ -94,12 +99,16 @@
     load(up_h, gu.at[pl.ds(nfeat, nfeat)])
     load(down_h, down)
 
-    rz[0] = rows[...]
+    for c in range(2):
+        rz[c, 0] = rows[:, c * half : (c + 1) * half]
     xin = tin[...].astype(F32)
     eye = iota((nfeat, nfeat), 0) == iota((nfeat, nfeat), 1)
     gain_col = jnp.sum(jnp.where(eye, gain[...].astype(F32), 0.0), axis=1, keepdims=True)
-    xf[0, 0] = (xin * gain_col).astype(BF16)
-    ss1[...] = jnp.sum((xin * xin).reshape(nfeat // 8, 8, ntok), axis=0)
+    xg = (xin * gain_col).astype(BF16)
+    xa[0, 0] = xg[:fh]
+    xb[0, 0] = xg[fh:]
+    squares = jnp.sum((xin * xin).reshape(nfeat // 8, 8, ntok), axis=0)
+    ss1[...] = squares
 
     barrier = pltpu.get_barrier_semaphore()
     peers = (
@@ -111,10 +120,14 @@
         pl.semaphore_signal(barrier, inc=1, device_id=device, device_id_type=MESH)
     pl.semaphore_wait(barrier, len(peers))
 
-    for d in range(1, nz):
-        start(rz.at[0], rz.at[d], ROWS_Z, d, z_peer(d)[1])
-    for d in range(1, nz):
-        start(xf.at[0, 0], xf.at[0, d], XG_Z, d, z_peer(d)[1])
+    relay = nz == 8
+    for c in range(2):
+        for d in (2, 6, 1, 7) if relay else range(1, nz):
+            start(rz.at[c, 0], rz.at[c, d], ROWS_Z0 + c, d, z_peer(d)[1])
+    for d in range(1, nk):
+        start(xa.at[0, 0], xa.at[0, d], XA_P, d, p_peer(d)[2])
+    for d in range(1, nz):
+        start(xb.at[0, 0], xb.at[0, d], XB_Z, d, z_peer(d)[1])
         start(ss1, ssz.at[d], SS_Z, d, z_peer(d)[1])
 
     for copy in loads[:NY]:
@@ -124,7 +137,26 @@
     mine = iota((nk, CAP, cap_z), 1) == (iota((nk, CAP, cap_z), 2) & (CAP - 1))
     target = jnp.sum(jnp.where(mine, slots.reshape(nk, CAP, cap_z), 0.0), axis=1)
     slot_z = (z + nz - lax.shift_right_logical(iota((nk, cap_z), 1), 4)) & (nz - 1)
-    sel[...] = target.astype(jnp.int32) + slot_z * trows
+    sel = target.astype(jnp.int32) + slot_z * trows
+    row_of = iota((nz * trows, cap_z), 0)
+    for k in range(nk):
+        hot[k] = (row_of == sel[k : k + 1]).astype(F32).astype(BF16)
+
+    if relay:
+        low, high = pl.ds(0, trows // 2), pl.ds(trows // 2, trows // 2)
+        for c in range(2):
+            stage = ROWS_Z0 + c
+            arrived(rz.at[c, 2], stage, 2)
+            start(rz.at[c, 2, low], rz.at[c, 4, low], stage, 4, z_peer(2)[1])
+            start(rz.at[c, 2], rz.at[c, 3], stage, 3, z_peer(1)[1])
+            arrived(rz.at[c, 6], stage, 6)
+            start(rz.at[c, 6, high], rz.at[c, 4, high], stage, 0, z_peer(6)[1])
+            start(rz.at[c, 6], rz.at[c, 5], stage, 5, z_peer(7)[1])
+
+    for d in range(1, nk):
+        arrived(xa.at[0, d], XA_P, d)
+    for d in range(1, nz):
+        start(xa.at[0], xa.at[d], XA_Z, d, z_peer(d)[1])
 
     for copy in loads[NY : NY + 1 + nk]:
         copy.wait()
@@ -134,30 +166,34 @@
         pred[k] = p
         stat[0, k : k + 1, :] = jnp.sum(p * p, axis=0, keepdims=True)
 
-    for d in range(1, nz):
-        arrived(rz.at[d], ROWS_Z, d)
-    rz_t = rz[...].reshape(nz * trows, width).T
-    row_of = iota((nz * trows, cap_z), 0)
-    for d in list(range(1, nk)) + [0]:
-        yy, xx, device = p_peer(d)
-        onehot = (row_of == sel[pl.ds(yy * nx + xx, 1), :]).astype(F32).astype(BF16)
-        picked = dot(rz_t, onehot, 1, 0).astype(BF16)
-        if d == 0:
-            tta[0] = picked
+    for c in range(2):
+        stage = ROWS_Z0 + c
+        if relay:
+            for d in (1, 7, 3, 5):
+                arrived(rz.at[c, d], stage, d)
+            arrived(rz.at[c, 4, low], stage, 4)
+            arrived(rz.at[c, 4, high], stage, 0)
         else:
-            tts[d] = picked
-            start(tts.at[d], tta.at[d], ROWS_P, d, device)
-
-    for d in range(1, nz):
-        arrived(xf.at[0, d], XG_Z, d)
+            for d in range(1, nz):
+                arrived(rz.at[c, d], stage, d)
+        rz_t = rz[c].reshape(nz * trows, half).T
+        for d in list(range(1, nk)) + [0]:
+            yy, xx, device = p_peer(d)
+            picked = dot(rz_t, hot[yy * nx + xx], 1, 0).astype(BF16)
+            if d == 0:
+                tta[c, 0] = picked
+            else:
+                tts[c, d] = picked
+                start(tts.at[c, d], tta.at[c, d], ROWS_P0 + c, d, device)
+
+    for d in range(1, nz):
+        arrived(xb.at[0, d], XB_Z, d)
         arrived(ssz.at[d], SS_Z, d)
-    squares = ss1[...]
-    for d in range(1, nz):
         squares += ssz[d]
     ss2[...] = squares
     for d in range(1, nk):
         device = p_peer(d)[2]
-        start(xf.at[0], xf.at[d], XG_P, d, device)
+        start(xb.at[0], xb.at[d], XB_P, d, device)
         start(ss2, ssp.at[d], SS_P, d, device)
 
     r = iota((ds, 1), 0).astype(F32)
@@ -170,19 +206,24 @@
         xt[:, k * cap_z : (k + 1) * cap_z] = dot(order, xv[k].reshape(cap_z, ds), 1, 1).astype(BF16)
 
     for d in range(nk):
-        if d:
-            arrived(tta.at[d], ROWS_P, d)
-        t = tta[d].astype(F32)
-        stat[1, d : d + 1, :] = jnp.sum(t * t, axis=0, keepdims=True)
-        stat[2, d : d + 1, :] = jnp.sum(t * pred[d], axis=0, keepdims=True)
+        tt_sum = pt_sum = 0.0
+        for c in range(2):
+            if d:
+                arrived(tta.at[c, d], ROWS_P0 + c, d)
+            t = tta[c, d].astype(F32)
+            tt_sum += jnp.sum(t * t, axis=0, keepdims=True)
+            pt_sum += jnp.sum(t * pred[d, c * half : (c + 1) * half], axis=0, keepdims=True)
+        stat[1, d : d + 1, :] = tt_sum
+        stat[2, d : d + 1, :] = pt_sum
     for d in range(1, groups):
         start(stat, stats.at[d], STATS, d, g_peer(d))
 
     for d in range(1, nk):
-        arrived(xf.at[d], XG_P, d)
         arrived(ssp.at[d], SS_P, d)
-    for d in range(1, nk):
         squares += ssp[d]
+        arrived(xb.at[d], XB_P, d)
+    for d in range(1, nz):
+        arrived(xa.at[d], XA_Z, d)
     total = jnp.sum(squares, axis=0, keepdims=True)
     scale = lax.rsqrt(total * (1.0 / (ndp * nfeat)) + 1e-05)
     for copy in loads[NY + 1 + nk :]:
@@ -190,7 +231,9 @@
     for d in range(nk):
         yy, xx = p_source(d)
         for dz in range(nz):
-            xn[yy * nz + (z + nz - dz) % nz, xx] = xf[d, dz]
+            place = yy * nz + (z + nz - dz) % nz
+            xn[place, xx, :fh] = xa[dz, d]
+            xn[place, xx, fh:] = xb[d, dz]
     h = dot(gu[...], xn[...].reshape(ndp * nfeat, ntok), 1, 0)
     gate, up = h[:nfeat] * scale, h[nfeat:] * scale
     hidden = (gate * jax.nn.sigmoid(gate) * up).astype(BF16)
@@ -199,10 +242,14 @@
         m = dot(down[:, yy * per_y : (yy + 1) * per_y], hidden, 0, 0).reshape(nz, nx, nfeat, ntok)
         mix[pl.ds(yy * nz, nz)] = m
         for xx in range(nx):
-            mixb[xx, pl.ds(yy * nz, nz)] = m[:, xx].astype(BF16)
+            mixa[yy * nx + xx] = m[:, xx, :fh].astype(BF16)
+            mixb[:, yy * nx + xx] = m[:, xx, fh:].astype(BF16)
+    for d in range(1, nz):
+        zz, device = z_peer(d)
+        start(mixb.at[zz], mrb.at[d], MB_Z, d, device)
     for d in range(1, nk):
         yy, xx, device = p_peer(d)
-        start(mixb.at[xx, pl.ds(yy * nz, nz)], mr.at[d], MIX_P, d, device)
+        start(mixa.at[yy * nx + xx], mra.at[d], MA_P, d, device)
 
     for d in range(1, groups):
         arrived(stats.at[d], STATS, d)
@@ -224,7 +271,7 @@
     a, b = weight * pt * inv / pp, weight * inv
     for k in range(nk):
         dpt[:, k * cap_z : (k + 1) * cap_z] = (
-            a[k : k + 1] * pred[k] - b[k : k + 1] * tta[k].astype(F32)
+            a[k : k + 1] * pred[k] - b[k : k + 1] * tta[:, k].reshape(width, cap_z).astype(F32)
         ).astype(BF16)
     gw = dot(xt[...], dpt[...], 1, 1).reshape(nk, part, width)
     grad[...] = gw
@@ -233,16 +280,26 @@
         yy, xx, device = p_peer(d)
         start(gs.at[yy * nx + xx], gr.at[d], GRAD_P, d, device)
 
-    for d in range(1, nk):
-        arrived(mr.at[d], MIX_P, d)
-    m = mix[pl.ds(y * nz, nz), x]
-    for d in range(1, nk):
-        m += mr[d].astype(F32)
-    mzf[...] = m
-    mz[...] = m.astype(BF16)
+    m = mix[pl.ds(y * nz, nz), x, :fh]
+    for d in range(1, nk):
+        arrived(mra.at[d], MA_P, d)
+        m += mra[d].astype(F32)
+    mfa[...] = m
+    m2a[...] = m.astype(BF16)
     for d in range(1, nz):
         zz, device = z_peer(d)
-        start(mz.at[zz], mzr.at[d], MIX_Z, d, device)
+        start(m2a.at[zz], mr2a.at[d], MA_Z, d, device)
+    for yy in range(NY):
+        mfb[pl.ds(yy * nx, nx)] = mix[yy * nz + z, :, fh:]
+    m = mfb[...]
+    for d in range(1, nz):
+        arrived(mrb.at[d], MB_Z, d)
+        m += mrb[d].astype(F32)
+    mfb[...] = m
+    m2b[...] = m.astype(BF16)
+    for d in range(1, nk):
+        yy, xx, device = p_peer(d)
+        start(m2b.at[yy * nx + xx], mr2b.at[d], MB_P, d, device)
 
     for d in range(1, nk):
         arrived(lossp.at[d], LOSS_P, d)
@@ -268,11 +325,16 @@
         zz, device = z_peer(d)
         start(gz.at[zz], gzr.at[d], GRAD_Z, d, device)
 
-    m = xin + mzf[z]
-    for d in range(1, nz):
-        arrived(mzr.at[d], MIX_Z, d)
-        m += mzr[d].astype(F32)
-    tout[...] = m.astype(BF16)
+    m = xin[:fh] + mfa[z]
+    for d in range(1, nz):
+        arrived(mr2a.at[d], MA_Z, d)
+        m += mr2a[d].astype(F32)
+    tout[pl.ds(0, fh)] = m.astype(BF16)
+    m = xin[fh:] + mfb[me]
+    for d in range(1, nk):
+        arrived(mr2b.at[d], MB_P, d)
+        m += mr2b[d].astype(F32)
+    tout[pl.ds(fh, fh)] = m.astype(BF16)
 
     for d in range(1, nz):
         arrived(lossz.at[d], LOSS_Z, d)
@@ -312,16 +374,17 @@
         v((nk, nz, CAP, ds), BF16),
         v((ds, width), BF16),
         v((nk, CAP, ndp), jnp.int32),
-        v((nk, nz, nfeat, ntok), BF16),
+        v((nz, nk, nfeat // 2, ntok), BF16),
+        v((nk, nz, nfeat // 2, ntok), BF16),
         v((NY * nz, nx, nfeat, ntok), BF16),
         v((8, ntok), F32),
         v((8, ntok), F32),
         v((nz, 8, ntok), F32),
         v((nk, 8, ntok), F32),
-        v((nz, trows, width), BF16),
-        v((nk, cap_z), jnp.int32),
-        v((nk, width, cap_z), BF16),
-        v((nk, width, cap_z), BF16),
+        v((2, nz, trows, width // 2), BF16),
+        v((nk, nz * trows, cap_z), BF16),
+        v((2, nk, width // 2, cap_z), BF16),
+        v((2, nk, width // 2, cap_z), BF16),
         v((width, ds), BF16),
         v((ds, s_dev), BF16),
         v((nk, width, cap_z), F32),
@@ -340,11 +403,16 @@
         v((nk, nk, cap_z), F32),
         v((nz, nk, cap_z), F32),
         v((NY * nz, nx, nfeat, ntok), F32),
-        v((nx, NY * nz, nfeat, ntok), BF16),
-        v((nk, nz, nfeat, ntok), BF16),
-        v((nz, nfeat, ntok), F32),
-        v((nz, nfeat, ntok), BF16),
-        v((nz, nfeat, ntok), BF16),
+        v((nk, nz, nfeat // 2, ntok), BF16),
+        v((nz, nk, nfeat // 2, ntok), BF16),
+        v((nk, nz, nfeat // 2, ntok), BF16),
+        v((nz, nk, nfeat // 2, ntok), BF16),
+        v((nz, nfeat // 2, ntok), F32),
+        v((nk, nfeat // 2, ntok), F32),
+        v((nz, nfeat // 2, ntok), BF16),
+        v((nk, nfeat // 2, ntok), BF16),
+        v((nz, nfeat // 2, ntok), BF16),
+        v((nk, nfeat // 2, ntok), BF16),
         pltpu.SemaphoreType.DMA((STAGES, max(nk, nz, groups))),
         pltpu.SemaphoreType.DMA((STAGES, max(nk, nz, groups))),
         pltpu.SemaphoreType.DMA((NY + 4 + nk,)),
@@ -360,7 +428,7 @@
         out_specs=(vm, vm, sm),
         scratch_shapes=scratch,
         compiler_params=pltpu.CompilerParams(
-            collective_id=0, has_side_effects=True, vmem_limit_bytes=52 * 1024 * 1024
+            collective_id=0, has_side_effects=True, vmem_limit_bytes=60 * 1024 * 1024
         ),
         name="distill",
     )(

time: 95.8 us -> 78.6 us (0.82)
  the two profiles are of different devices: /device:TPU:2 before, /device:TPU:8 now
where the time goes in v2:
time: 78.6 us; the launch traced here: 78.3 us
  Pallas kernels  73.2 us (93%)
  local copies, waits for them, and re-layouts  2.7 us (3%)
  between operations  2.38 us (3%)
    pallas_call x1, Pallas kernels, on_device(): pl.pallas_call(functools.partial(kernel, nz, nx), out_shape=(jax.ShapeDty...  73.2 us
    unnamed x2, local copies, waits for them, and re-layouts  2.7 us

profile of v2, /device:TPU:8, one launch (start us, length us, event | category | flops | bytes accessed | tf_op | source)
XLA Modules:
  0.0 78.3 jit_solution(6140355952326318198)
XLA Ops:
  0.6 73.2 %distill.1 = (bf16[64,128]{1,0:T(8,128)(2,1)}, f32[12,512]{1,0:T(8,128)}, f32[1,1]{1,0:T(1,128)}) custom-call(bf16[64,128]{1,0:T(8,128)(2,1)} %bitcast.14, bf16[1,64]{1,0:T(2,128)(2,1)} %bitcast.16, bf16[64,512]{1,0:T(8,128)(2,1)} %rows.1, bf16[64,4096]{1,0:T(8,128)(2,1)} %bitcast.11, bf16[64,4096]{1,0:T(8,128)(2,1)} %bitcast.12, bf16[64,4096]{1,0:T(8,128)(2,1)} %down_h.1, ...), custom_call_target="tpu_custom_call" | custom-call | tf_op jit(solution)/shard_map/distill/pallas_call | solution.py:420
  73.9 1.3 %copy.16 = bf16[128,64]{0,1:T(8,128)(2,1)} copy(bf16[128,64]{0,1:T(8,128)(2,1)} %bitcast.15) | data formatting | bytes 32768
  75.2 1.4 %copy.17 = f32[12,512]{1,0:T(8,128)} copy(f32[12,512]{1,0:T(8,128)} %get-tuple-element.13) | data formatting | bytes 49152

commit v3 on v2

--- a/solution.py
+++ b/solution.py
@@ -120,15 +120,15 @@
         pl.semaphore_signal(barrier, inc=1, device_id=device, device_id_type=MESH)
     pl.semaphore_wait(barrier, len(peers))
 
+    for d in range(1, nz):
+        start(xb.at[0, 0], xb.at[0, d], XB_Z, d, z_peer(d)[1])
+        start(ss1, ssz.at[d], SS_Z, d, z_peer(d)[1])
     relay = nz == 8
     for c in range(2):
         for d in (2, 6, 1, 7) if relay else range(1, nz):
             start(rz.at[c, 0], rz.at[c, d], ROWS_Z0 + c, d, z_peer(d)[1])
     for d in range(1, nk):
         start(xa.at[0, 0], xa.at[0, d], XA_P, d, p_peer(d)[2])
-    for d in range(1, nz):
-        start(xb.at[0, 0], xb.at[0, d], XB_Z, d, z_peer(d)[1])
-        start(ss1, ssz.at[d], SS_Z, d, z_peer(d)[1])
 
     for copy in loads[:NY]:
         copy.wait()
@@ -141,6 +141,16 @@
     row_of = iota((nz * trows, cap_z), 0)
     for k in range(nk):
         hot[k] = (row_of == sel[k : k + 1]).astype(F32).astype(BF16)
+
+    for d in range(1, nz):
+        arrived(xb.at[0, d], XB_Z, d)
+        arrived(ssz.at[d], SS_Z, d)
+        squares += ssz[d]
+    ss2[...] = squares
+    for d in range(1, nk):
+        device = p_peer(d)[2]
+        start(xb.at[0], xb.at[d], XB_P, d, device)
+        start(ss2, ssp.at[d], SS_P, d, device)
 
     if relay:
         low, high = pl.ds(0, trows // 2), pl.ds(trows // 2, trows // 2)
@@ -185,16 +195,6 @@
             else:
                 tts[c, d] = picked
                 start(tts.at[c, d], tta.at[c, d], ROWS_P0 + c, d, device)
-
-    for d in range(1, nz):
-        arrived(xb.at[0, d], XB_Z, d)
-        arrived(ssz.at[d], SS_Z, d)
-        squares += ssz[d]
-    ss2[...] = squares
-    for d in range(1, nk):
-        device = p_peer(d)[2]
-        start(xb.at[0], xb.at[d], XB_P, d, device)
-        start(ss2, ssp.at[d], SS_P, d, device)
 
     r = iota((ds, 1), 0).astype(F32)
     rk = jnp.floor((r + 0.5) / part)

time: 78.6 us -> 74.3 us (0.945)
  the two profiles are of different devices: /device:TPU:8 before, /device:TPU:10 now
where the time goes in v3:
time: 74.3 us; the launch traced here: 74 us
  Pallas kernels  68.9 us (93%)
  local copies, waits for them, and re-layouts  2.7 us (4%)
  between operations  2.38 us (3%)
    pallas_call x1, Pallas kernels, on_device(): pl.pallas_call(functools.partial(kernel, nz, nx), out_shape=(jax.ShapeDty...  68.9 us
    unnamed x2, local copies, waits for them, and re-layouts  2.7 us

profile of v3, /device:TPU:10, one launch (start us, length us, event | category | flops | bytes accessed | tf_op | source)
XLA Modules:
  0.0 74.0 jit_solution(8020044887777631875)
XLA Ops:
  0.6 68.9 %distill.1 = (bf16[64,128]{1,0:T(8,128)(2,1)}, f32[12,512]{1,0:T(8,128)}, f32[1,1]{1,0:T(1,128)}) custom-call(bf16[64,128]{1,0:T(8,128)(2,1)} %bitcast.14, bf16[1,64]{1,0:T(2,128)(2,1)} %bitcast.16, bf16[64,512]{1,0:T(8,128)(2,1)} %rows.1, bf16[64,4096]{1,0:T(8,128)(2,1)} %bitcast.11, bf16[64,4096]{1,0:T(8,128)(2,1)} %bitcast.12, bf16[64,4096]{1,0:T(8,128)(2,1)} %down_h.1, ...), custom_call_target="tpu_custom_call" | custom-call | tf_op jit(solution)/shard_map/distill/pallas_call | solution.py:420
  69.6 1.3 %copy.16 = bf16[128,64]{0,1:T(8,128)(2,1)} copy(bf16[128,64]{0,1:T(8,128)(2,1)} %bitcast.15) | data formatting | bytes 32768
  70.9 1.4 %copy.17 = f32[12,512]{1,0:T(8,128)} copy(f32[12,512]{1,0:T(8,128)} %get-tuple-element.13) | data formatting | bytes 49152

commit v4 on v3

--- a/solution.py
+++ b/solution.py
@@ -9,15 +9,17 @@
 
 NY = 2
 CAP = 16
+FA = 32
+MA = 48
 MESH = pl.DeviceIdType.MESH
 F32 = jnp.float32
 BF16 = jnp.bfloat16
 
 (
     XA_P, XA_Z, XB_Z, XB_P, SS_Z, SS_P, ROWS_Z0, ROWS_Z1, ROWS_P0, ROWS_P1, STATS,
-    MA_P, MA_Z, MB_Z, MB_P, GRAD_P, GRAD_Z, LOSS_P, LOSS_Z,
-) = range(19)
-STAGES = 19
+    MA_P, MA_Z, MB_Z, MB_P, GA_P, GA_Z, GB_Z, GB_P, LOSS_P, LOSS_Z,
+) = range(21)
+STAGES = 21
 
 
 def dot(a, b, ca, cb):
@@ -33,7 +35,7 @@
     tin, gain, rows, gate_h, up_h, down_h, x_h, w_h, tr_h, counts,
     tout, gout, loss_out,
     gu, down, xv, wv, tr, xa, xb, xn, ss1, ss2, ssz, ssp, rz, hot, tts, tta, wt, xt, pred, stat, stats, dpt,
-    grad, gs, gr, gacc, gzf, gz, gzr, loss1, loss2, lossp, lossz,
+    grad, gs, gr, gacc, gz, gzr, gb, gbs, gbr, gb2, gbr2, loss1, loss2, lossp, lossz,
     mix, mixa, mixb, mra, mrb, mfa, mfb, m2a, m2b, mr2a, mr2b,
     send, recv, local,
 ):
@@ -50,7 +52,9 @@
     tokens = cap_z * nk
     part = ds // nk
     out_rows = part // nz
-    half, fh = width // 2, nfeat // 2
+    half = width // 2
+    fa, ma = FA, MA
+    wa = width - width // 4
 
     def z_peer(d):
         zz = (z + d) % nz
@@ -105,8 +109,8 @@
     eye = iota((nfeat, nfeat), 0) == iota((nfeat, nfeat), 1)
     gain_col = jnp.sum(jnp.where(eye, gain[...].astype(F32), 0.0), axis=1, keepdims=True)
     xg = (xin * gain_col).astype(BF16)
-    xa[0, 0] = xg[:fh]
-    xb[0, 0] = xg[fh:]
+    xa[0, 0] = xg[:fa]
+    xb[0, 0] = xg[fa:]
     squares = jnp.sum((xin * xin).reshape(nfeat // 8, 8, ntok), axis=0)
     ss1[...] = squares
 
@@ -197,10 +201,17 @@
                 start(tts.at[c, d], tta.at[c, d], ROWS_P0 + c, d, device)
 
     r = iota((ds, 1), 0).astype(F32)
-    rk = jnp.floor((r + 0.5) / part)
-    rz_ = jnp.floor((r - rk * part + 0.5) / out_rows)
-    ry = jnp.floor((rk + 0.5) / nx)
-    column = ((ry * nz + rz_) * nx + (rk - ry * nx)) * out_rows + (r - rk * part - rz_ * out_rows)
+    rd = jnp.floor((r + 0.5) / part)
+    rz_ = jnp.floor((r - rd * part + 0.5) / out_rows)
+    ry = jnp.floor((rd + 0.5) / nx)
+
+    def turn(v, n):
+        return v - jnp.where(v > n - 0.5, float(n), 0.0)
+
+    oy = turn(ry + y.astype(F32), NY)
+    ox = turn(rd - ry * nx + x.astype(F32), nx)
+    oz = turn(rz_ + z.astype(F32), nz)
+    column = ((oy * nz + oz) * nx + ox) * out_rows + (r - rd * part - rz_ * out_rows)
     order = (column == iota((ds, ds), 1).astype(F32)).astype(F32).astype(BF16)
     for k in range(nk):
         xt[:, k * cap_z : (k + 1) * cap_z] = dot(order, xv[k].reshape(cap_z, ds), 1, 1).astype(BF16)
@@ -232,8 +243,8 @@
         yy, xx = p_source(d)
         for dz in range(nz):
             place = yy * nz + (z + nz - dz) % nz
-            xn[place, xx, :fh] = xa[dz, d]
-            xn[place, xx, fh:] = xb[d, dz]
+            xn[place, xx, :fa] = xa[dz, d]
+            xn[place, xx, fa:] = xb[d, dz]
     h = dot(gu[...], xn[...].reshape(ndp * nfeat, ntok), 1, 0)
     gate, up = h[:nfeat] * scale, h[nfeat:] * scale
     hidden = (gate * jax.nn.sigmoid(gate) * up).astype(BF16)
@@ -242,8 +253,8 @@
         m = dot(down[:, yy * per_y : (yy + 1) * per_y], hidden, 0, 0).reshape(nz, nx, nfeat, ntok)
         mix[pl.ds(yy * nz, nz)] = m
         for xx in range(nx):
-            mixa[yy * nx + xx] = m[:, xx, :fh].astype(BF16)
-            mixb[:, yy * nx + xx] = m[:, xx, fh:].astype(BF16)
+            mixa[yy * nx + xx] = m[:, xx, :ma].astype(BF16)
+            mixb[:, yy * nx + xx] = m[:, xx, ma:].astype(BF16)
     for d in range(1, nz):
         zz, device = z_peer(d)
         start(mixb.at[zz], mrb.at[d], MB_Z, d, device)
@@ -273,14 +284,24 @@
         dpt[:, k * cap_z : (k + 1) * cap_z] = (
             a[k : k + 1] * pred[k] - b[k : k + 1] * tta[:, k].reshape(width, cap_z).astype(F32)
         ).astype(BF16)
-    gw = dot(xt[...], dpt[...], 1, 1).reshape(nk, part, width)
-    grad[...] = gw
-    gs[...] = gw.astype(BF16)
-    for d in range(1, nk):
-        yy, xx, device = p_peer(d)
-        start(gs.at[yy * nx + xx], gr.at[d], GRAD_P, d, device)
-
-    m = mix[pl.ds(y * nz, nz), x, :fh]
+    for first in range(0, nk, nk // 2):
+        many = nk // 2 * part
+        gw = dot(xt[first * part : first * part + many], dpt[...], 1, 1)
+        gb[first * part : first * part + many] = gw[:, wa:]
+        for d in range(first, first + nk // 2):
+            piece = gw[(d - first) * part : (d - first + 1) * part, :wa]
+            if d == 0:
+                grad[...] = piece
+            else:
+                gs[d] = piece.astype(BF16)
+                start(gs.at[d], gr.at[d], GA_P, d, p_peer(d)[2])
+    gb[pl.ds(ds, 16)] = jnp.zeros((16, width - wa), F32)
+    for dz in range(1, nz):
+        for d in range(nk):
+            gbs[dz, d] = gb[pl.ds(d * part + dz * out_rows, 16)].astype(BF16)
+        start(gbs.at[dz], gbr.at[dz], GB_Z, dz, z_peer(dz)[1])
+
+    m = mix[pl.ds(y * nz, nz), x, :ma]
     for d in range(1, nk):
         arrived(mra.at[d], MA_P, d)
         m += mra[d].astype(F32)
@@ -289,8 +310,18 @@
     for d in range(1, nz):
         zz, device = z_peer(d)
         start(m2a.at[zz], mr2a.at[d], MA_Z, d, device)
+    acc = grad[...]
+    for d in range(1, nk):
+        arrived(gr.at[d], GA_P, d)
+        acc += gr[d].astype(F32)
+    gacc[pl.ds(0, part)] = acc
+    gacc[pl.ds(part, 16)] = jnp.zeros((16, wa), F32)
+    for dz in range(1, nz):
+        gz[dz] = gacc[pl.ds(dz * out_rows, 16)].astype(BF16)
+        start(gz.at[dz], gzr.at[dz], GA_Z, dz, z_peer(dz)[1])
+
     for yy in range(NY):
-        mfb[pl.ds(yy * nx, nx)] = mix[yy * nz + z, :, fh:]
+        mfb[pl.ds(yy * nx, nx)] = mix[yy * nz + z, :, ma:]
     m = mfb[...]
     for d in range(1, nz):
         arrived(mrb.at[d], MB_Z, d)
@@ -301,6 +332,15 @@
         yy, xx, device = p_peer(d)
         start(m2b.at[yy * nx + xx], mr2b.at[d], MB_P, d, device)
 
+    sums_b = [gb[pl.ds(d * part, 16)] for d in range(nk)]
+    for dz in range(1, nz):
+        arrived(gbr.at[dz], GB_Z, dz)
+        for d in range(nk):
+            sums_b[d] += gbr[dz, d].astype(F32)
+    for d in range(1, nk):
+        gb2[d] = sums_b[d].astype(BF16)
+        start(gb2.at[d], gbr2.at[d], GB_P, d, p_peer(d)[2])
+
     for d in range(1, nk):
         arrived(lossp.at[d], LOSS_P, d)
     part_loss = loss1[...]
@@ -310,42 +350,32 @@
     for d in range(1, nz):
         start(loss2, lossz.at[d], LOSS_Z, d, z_peer(d)[1])
 
-    for d in range(1, nk):
-        arrived(gr.at[d], GRAD_P, d)
-    acc = grad[me]
-    for d in range(1, nk):
-        acc += gr[d].astype(F32)
-    gacc[pl.ds(0, part)] = acc
-    gacc[pl.ds(part, 16)] = jnp.zeros((16, width), F32)
-    for zz in range(nz):
-        piece = gacc[pl.ds(zz * out_rows, 16)]
-        gzf[zz] = piece
-        gz[zz] = piece.astype(BF16)
-    for d in range(1, nz):
-        zz, device = z_peer(d)
-        start(gz.at[zz], gzr.at[d], GRAD_Z, d, device)
-
-    m = xin[:fh] + mfa[z]
+    m = xin[:ma] + mfa[z]
     for d in range(1, nz):
         arrived(mr2a.at[d], MA_Z, d)
         m += mr2a[d].astype(F32)
-    tout[pl.ds(0, fh)] = m.astype(BF16)
-    m = xin[fh:] + mfb[me]
+    tout[pl.ds(0, ma)] = m.astype(BF16)
+    m = xin[ma:] + mfb[me]
     for d in range(1, nk):
         arrived(mr2b.at[d], MB_P, d)
         m += mr2b[d].astype(F32)
-    tout[pl.ds(fh, fh)] = m.astype(BF16)
+    tout[pl.ds(ma, nfeat - ma)] = m.astype(BF16)
 
     for d in range(1, nz):
         arrived(lossz.at[d], LOSS_Z, d)
         part_loss += lossz[d]
     loss_out[0, 0] = jnp.sum(part_loss) / count.astype(F32)
 
-    acc = gzf[z]
-    for d in range(1, nz):
-        arrived(gzr.at[d], GRAD_Z, d)
-        acc += gzr[d].astype(F32)
-    gout[...] = acc[:out_rows]
+    acc = gacc[pl.ds(0, 16)]
+    for dz in range(1, nz):
+        arrived(gzr.at[dz], GA_Z, dz)
+        acc += gzr[dz].astype(F32)
+    gout[:, :wa] = acc[:out_rows]
+    acc = sums_b[0]
+    for d in range(1, nk):
+        arrived(gbr2.at[d], GB_P, d)
+        acc += gbr2[d].astype(F32)
+    gout[:, wa:] = acc[:out_rows]
 
     for copy in started:
         copy.wait_send()
@@ -364,6 +394,7 @@
     part = ds // nk
     out_rows = part // nz
     d_model = ndp * nfeat
+    wa = width - width // 4
     vm = pl.BlockSpec(memory_space=pltpu.VMEM)
     hbm = pl.BlockSpec(memory_space=pl.ANY)
     sm = pl.BlockSpec(memory_space=pltpu.SMEM)
@@ -374,8 +405,8 @@
         v((nk, nz, CAP, ds), BF16),
         v((ds, width), BF16),
         v((nk, CAP, ndp), jnp.int32),
-        v((nz, nk, nfeat // 2, ntok), BF16),
-        v((nk, nz, nfeat // 2, ntok), BF16),
+        v((nz, nk, FA, ntok), BF16),
+        v((nk, nz, nfeat - FA, ntok), BF16),
         v((NY * nz, nx, nfeat, ntok), BF16),
         v((8, ntok), F32),
         v((8, ntok), F32),
@@ -391,28 +422,32 @@
         v((3, nk, cap_z), F32),
         v((groups, 3, nk, cap_z), F32),
         v((width, s_dev), BF16),
-        v((nk, part, width), F32),
-        v((nk, part, width), BF16),
-        v((nk, part, width), BF16),
-        v((part + 16, width), F32),
-        v((nz, 16, width), F32),
-        v((nz, 16, width), BF16),
-        v((nz, 16, width), BF16),
+        v((part, wa), F32),
+        v((nk, part, wa), BF16),
+        v((nk, part, wa), BF16),
+        v((part + 16, wa), F32),
+        v((nz, 16, wa), BF16),
+        v((nz, 16, wa), BF16),
+        v((ds + 16, width - wa), F32),
+        v((nz, nk, 16, width - wa), BF16),
+        v((nz, nk, 16, width - wa), BF16),
+        v((nk, 16, width - wa), BF16),
+        v((nk, 16, width - wa), BF16),
         v((nk, cap_z), F32),
         v((nk, cap_z), F32),
         v((nk, nk, cap_z), F32),
         v((nz, nk, cap_z), F32),
         v((NY * nz, nx, nfeat, ntok), F32),
-        v((nk, nz, nfeat // 2, ntok), BF16),
-        v((nz, nk, nfeat // 2, ntok), BF16),
-        v((nk, nz, nfeat // 2, ntok), BF16),
-        v((nz, nk, nfeat // 2, ntok), BF16),
-        v((nz, nfeat // 2, ntok), F32),
-        v((nk, nfeat // 2, ntok), F32),
-        v((nz, nfeat // 2, ntok), BF16),
-        v((nk, nfeat // 2, ntok), BF16),
-        v((nz, nfeat // 2, ntok), BF16),
-        v((nk, nfeat // 2, ntok), BF16),
+        v((nk, nz, MA, ntok), BF16),
+        v((nz, nk, nfeat - MA, ntok), BF16),
+        v((nk, nz, MA, ntok), BF16),
+        v((nz, nk, nfeat - MA, ntok), BF16),
+        v((nz, MA, ntok), F32),
+        v((nk, nfeat - MA, ntok), F32),
+        v((nz, MA, ntok), BF16),
+        v((nk, nfeat - MA, ntok), BF16),
+        v((nz, MA, ntok), BF16),
+        v((nk, nfeat - MA, ntok), BF16),
         pltpu.SemaphoreType.DMA((STAGES, max(nk, nz, groups))),
         pltpu.SemaphoreType.DMA((STAGES, max(nk, nz, groups))),
         pltpu.SemaphoreType.DMA((NY + 4 + nk,)),

time: 74.3 us -> 73.2 us (0.985)
  the two profiles are of different devices: /device:TPU:10 before, /device:TPU:8 now
where the time goes in v4:
time: 73.2 us; the launch traced here: 72.8 us
  Pallas kernels  67.7 us (92%)
  local copies, waits for them, and re-layouts  2.7 us (4%)
  between operations  2.38 us (3%)
    pallas_call x1, Pallas kernels, on_device(): pl.pallas_call(functools.partial(kernel, nz, nx), out_shape=(jax.ShapeDty...  67.7 us
    unnamed x2, local copies, waits for them, and re-layouts  2.7 us

profile of v4, /device:TPU:8, one launch (start us, length us, event | category | flops | bytes accessed | tf_op | source)
XLA Modules:
  0.0 72.8 jit_solution(3219699352853631327)
XLA Ops:
  0.6 67.7 %distill.1 = (bf16[64,128]{1,0:T(8,128)(2,1)}, f32[12,512]{1,0:T(8,128)}, f32[1,1]{1,0:T(1,128)}) custom-call(bf16[64,128]{1,0:T(8,128)(2,1)} %bitcast.14, bf16[1,64]{1,0:T(2,128)(2,1)} %bitcast.16, bf16[64,512]{1,0:T(8,128)(2,1)} %rows.1, bf16[64,4096]{1,0:T(8,128)(2,1)} %bitcast.11, bf16[64,4096]{1,0:T(8,128)(2,1)} %bitcast.12, bf16[64,4096]{1,0:T(8,128)(2,1)} %down_h.1, ...), custom_call_target="tpu_custom_call" | custom-call | tf_op jit(solution)/shard_map/distill/pallas_call | solution.py:455
  68.3 1.3 %copy.16 = bf16[128,64]{0,1:T(8,128)(2,1)} copy(bf16[128,64]{0,1:T(8,128)(2,1)} %bitcast.15) | data formatting | bytes 32768
  69.7 1.4 %copy.17 = f32[12,512]{1,0:T(8,128)} copy(f32[12,512]{1,0:T(8,128)} %get-tuple-element.13) | data formatting | bytes 49152

commit v5 on v4

--- a/solution.py
+++ b/solution.py
@@ -255,12 +255,12 @@
         for xx in range(nx):
             mixa[yy * nx + xx] = m[:, xx, :ma].astype(BF16)
             mixb[:, yy * nx + xx] = m[:, xx, ma:].astype(BF16)
+    for d in range(1, nk):
+        yy, xx, device = p_peer(d)
+        start(mixa.at[yy * nx + xx], mra.at[d], MA_P, d, device)
     for d in range(1, nz):
         zz, device = z_peer(d)
         start(mixb.at[zz], mrb.at[d], MB_Z, d, device)
-    for d in range(1, nk):
-        yy, xx, device = p_peer(d)
-        start(mixa.at[yy * nx + xx], mra.at[d], MA_P, d, device)
 
     for d in range(1, groups):
         arrived(stats.at[d], STATS, d)

time: 73.2 us -> 73.2 us (level)
  no operation moved by 1% of the time
where the time goes in v5:
time: 73.2 us; the launch traced here: 72.8 us
  Pallas kernels  67.7 us (92%)
  local copies, waits for them, and re-layouts  2.7 us (4%)
  between operations  2.38 us (3%)
    pallas_call x1, Pallas kernels, on_device(): pl.pallas_call(functools.partial(kernel, nz, nx), out_shape=(jax.ShapeDty...  67.7 us
    unnamed x2, local copies, waits for them, and re-layouts  2.7 us

profile of v5, /device:TPU:8, one launch (start us, length us, event | category | flops | bytes accessed | tf_op | source)
XLA Modules:
  0.0 72.8 jit_solution(9375733991813788699)
XLA Ops:
  0.6 67.7 %distill.1 = (bf16[64,128]{1,0:T(8,128)(2,1)}, f32[12,512]{1,0:T(8,128)}, f32[1,1]{1,0:T(1,128)}) custom-call(bf16[64,128]{1,0:T(8,128)(2,1)} %bitcast.14, bf16[1,64]{1,0:T(2,128)(2,1)} %bitcast.16, bf16[64,512]{1,0:T(8,128)(2,1)} %rows.1, bf16[64,4096]{1,0:T(8,128)(2,1)} %bitcast.11, bf16[64,4096]{1,0:T(8,128)(2,1)} %bitcast.12, bf16[64,4096]{1,0:T(8,128)(2,1)} %down_h.1, ...), custom_call_target="tpu_custom_call" | custom-call | tf_op jit(solution)/shard_map/distill/pallas_call | solution.py:455
  68.4 1.3 %copy.16 = bf16[128,64]{0,1:T(8,128)(2,1)} copy(bf16[128,64]{0,1:T(8,128)(2,1)} %bitcast.15) | data formatting | bytes 32768
  69.7 1.4 %copy.17 = f32[12,512]{1,0:T(8,128)} copy(f32[12,512]{1,0:T(8,128)} %get-tuple-element.13) | data formatting | bytes 49152
